TPU v7x, 32 devices: a whole 2x2x4 slice. The times are simulated.
32 devices in a mesh: table: 2 (over x), image: 16 (over z, y, core).
Axes of the slice: x: 2, y: 2, z: 4, core: 2. Of those that a mesh axis runs over, the one named last changes fastest.
Arguments:
- traces: bfloat16 [512, 1920], P(('table', 'image')), may hold values from -6 to 6
- aperture: int32 [512, 4], P(('table', 'image')), may hold values from 0 to 15, all different within a row; in each aligned block of 16 rows (0 to 15, 16 to 31, ...) at most 8 rows name the same one
- bucket: int32 [512], P(('table', 'image')), may hold values from 0 to 3
- table_node: int32 [512, 4], P(('table', 'image')), may hold values from 0 to 15
- entry_gain: bfloat16 [512, 4], P(('table', 'image')), may hold values from 0.5 to 2
- travel: float32 [16, 16, 1024], P('image', None, 'table'), may hold values from 1 to 1918
- spread: float32 [16, 16, 1024], P('image', None, 'table'), may hold values from 0.1 to 1
Outputs:
- image: float32 [16, 1024], P('image', 'table')
Inputs may be any that keep to these rules, and one draw needn't show every extreme that they name: `aperture`: each trace names 4 different tiles. Among the 16 traces of one device at most 8 name the same tile, and in every draw some tile is named by exactly 8 of them.
All inputs are finite; a program needn't handle non-finite values.
Results may differ from a plain program's by a relative error of at most 0.0024.
Values may be sent and summed in bfloat16 or wider, within the bound.
A program may use at most 128 MiB of HBM per device.

v0:
```python
import math
import jax
import jax.numpy as jnp
from jax import lax
from jax.sharding import PartitionSpec as P

max_lag = 7


def antialias(trace_rows, filter_index):
    half_width = (2 + 2 * filter_index).astype(jnp.float32)[..., None]
    length = trace_rows.shape[-1]
    widths = [(0, 0)] * (trace_rows.ndim - 1) + [(max_lag, max_lag)]
    padded = jnp.pad(trace_rows, widths)
    summed = jnp.zeros(trace_rows.shape, jnp.float32)
    for sample_lag in range(-max_lag, max_lag + 1):
        ramp_weight = jnp.maximum(half_width - abs(sample_lag), 0.0) / (half_width * half_width)
        window = lax.slice_in_dim(
            padded, max_lag + sample_lag, max_lag + sample_lag + length, axis=trace_rows.ndim - 1
        )
        summed = summed + ramp_weight * window
    return summed


def interpolate(stack_tile, travel_tile, spread_tile):
    floor_value = jnp.floor(travel_tile)
    fraction = travel_tile - floor_value
    lower_index = floor_value.astype(jnp.int32)
    shifted = jnp.pad(stack_tile[:, 1:], ((0, 0), (0, 1)))
    paired = jnp.stack([stack_tile, shifted], axis=-1)
    picked = jnp.take_along_axis(paired, lower_index[:, :, None], axis=1)
    lower_value = picked[:, :, 0]
    upper_value = picked[:, :, 1]
    return jnp.sum(spread_tile * ((1.0 - fraction) * lower_value + fraction * upper_value), axis=0)


def per_device(traces, aperture, bucket, table_node, entry_gain, travel, spread):
    tiles = lax.axis_size("image")
    groups = lax.axis_size("table")
    trace_count, samples = traces.shape
    aper_count = aperture.shape[1]
    node_count = travel.shape[1]
    capacity = max(2, 2 * trace_count * aper_count // tiles)
    entries = trace_count * aper_count
    destination = aperture.reshape(entries)
    member = (destination[:, None] == jnp.arange(tiles, dtype=jnp.int32)[None, :]).astype(jnp.int32)
    earlier = jnp.cumsum(member, axis=0) - member
    slot_index = jnp.sum(earlier * member, axis=1)
    source_row = jnp.arange(entries, dtype=jnp.int32) // aper_count
    flat_nodes = table_node.reshape(entries)
    flat_gains = entry_gain.reshape(entries)
    node_slots = jnp.zeros((capacity, tiles), jnp.int32).at[slot_index, destination].set(flat_nodes)
    raw_slots = (
        jnp.zeros((capacity, tiles, samples), jnp.bfloat16)
        .at[slot_index, destination]
        .set(traces[source_row])
    )
    gain_slots = (
        jnp.zeros((capacity, tiles), jnp.bfloat16).at[slot_index, destination].set(flat_gains)
    )
    filter_slots = (
        jnp.zeros((capacity, tiles), jnp.int32).at[slot_index, destination].set(bucket[source_row])
    )
    raw_part = lax.all_to_all(raw_slots, "image", split_axis=1, concat_axis=1, tiled=True)
    gain_part = lax.all_to_all(gain_slots, "image", split_axis=1, concat_axis=1, tiled=True)
    filter_part = lax.all_to_all(filter_slots, "image", split_axis=1, concat_axis=1, tiled=True)
    node_part = lax.all_to_all(node_slots, "image", split_axis=1, concat_axis=1, tiled=True)
    filtered = antialias(raw_part.astype(jnp.float32), filter_part)
    weighted = (gain_part.astype(jnp.float32)[..., None] * filtered).astype(jnp.bfloat16)
    slot_total = tiles * capacity
    flat_values = weighted.reshape(slot_total, samples)
    node_member = (
        node_part.reshape(slot_total)[:, None] == jnp.arange(node_count, dtype=jnp.int32)[None, :]
    ).astype(jnp.bfloat16)
    stack = lax.dot_general(
        node_member, flat_values, (((0,), (0,)), ((), ())), preferred_element_type=jnp.float32
    )
    scale = 1.0 / math.sqrt(trace_count * groups * aper_count)
    summed_stack = lax.psum(stack, "table")
    return (interpolate(summed_stack, travel[0], spread[0]) * scale)[None, :]


def solution(mesh):
    in_specs = (
        P(("table", "image"), None),
        P(("table", "image"), None),
        P(("table", "image")),
        P(("table", "image"), None),
        P(("table", "image"), None),
        P("image", None, "table"),
        P("image", None, "table"),
    )
    out_specs = P("image", "table")
    return jax.shard_map(
        per_device, mesh=mesh, in_specs=in_specs, out_specs=out_specs, check_vma=False
    )
```

profile of v0, /device:TPU:0, one launch (start us, length us, event | category | flops | bytes accessed | tf_op | source)
XLA Modules:
  0.0 235.3 jit_solution(4942274203572084065)
XLA Ops:
  6.5 0.8 copy.41
  7.6 0.1 reduce_window_sum.11
  7.7 0.2 select_reduce_fusion
  7.8 0.8 copy.46
  8.6 0.1 reshape.206
  8.7 3.5 %scatter_fusion.1 = bf16[8,16]{1,0:T(8,128)(2,1)S(1)} fusion(bf16[8,16]{1,0:T(8,128)(2,1)S(1)} %broadcast_in_dim.11, s32[64]{0:T(128)S(1)} %fusion.25, bf16[64]{0:T(256)(128)(2,1)S(1)} %reshape.206), kind=kCustom, calls=%fused_computation.4 | custom fusion | bytes 896 | tf_op jit(solution)/shard_map/scatter | solution.py:59
  12.3 0.7 copy.47
  12.9 7.4 %all-to-all-start.1 = ((bf16[8,16,1]{0,2,1:T(2,128)(2,1)}), bf16[8,16,1]{0,2,1:T(2,128)(2,1)S(1)}, u32[]{:S(2)}, u32[]{:S(2)}) async-start(bf16[8,16,1]{0,2,1:T(2,128)(2,1)} %copy.47), calls=%async_computation.1 | async-start | bytes 16384 | tf_op jit(solution)/shard_map/all_to_all | solution.py:65
  20.4 1.4 gather_fusion
  21.8 3.5 %scatter_fusion.2 = s32[8,16]{1,0:T(8,128)S(1)} fusion(s32[8,16]{1,0:T(8,128)S(1)} %broadcast.222.clone, s32[64]{0:T(128)S(1)} %fusion.25, s32[64]{0:T(128)S(1)} %gather_fusion), kind=kCustom, calls=%fused_computation.5 | custom fusion | bytes 1280 | tf_op jit(solution)/shard_map/scatter | solution.py:62
  25.3 0.7 copy.49
  25.9 0.8 all-to-all-done.1
  26.7 5.2 %all-to-all-start.2 = ((s32[8,16,1]{0,2,1:T(1,128)}), s32[8,16,1]{0,2,1:T(1,128)S(1)}, u32[]{:S(2)}, u32[]{:S(2)}) async-start(s32[8,16,1]{0,2,1:T(1,128)} %copy.49), calls=%async_computation.2 | async-start | bytes 16384 | tf_op jit(solution)/shard_map/all_to_all | solution.py:66
  31.9 0.8 copy.43
  32.8 3.5 %scatter_fusion = s32[8,16]{1,0:T(8,128)S(1)} fusion(s32[8,16]{1,0:T(8,128)S(1)} %broadcast.222.clone.1, s32[64]{0:T(128)S(1)} %fusion.25, s32[64]{0:T(128)S(1)} %reshape.200), kind=kCustom, calls=%fused_computation.3 | custom fusion | bytes 1280 | tf_op jit(solution)/shard_map/scatter | solution.py:52
  36.3 0.7 copy.44
  36.9 1.4 all-to-all-done.2
  38.4 4.6 %all-to-all-start = ((s32[8,16,1]{0,2,1:T(1,128)}), s32[8,16,1]{0,2,1:T(1,128)S(1)}, u32[]{:S(2)}, u32[]{:S(2)}) async-start(s32[8,16,1]{0,2,1:T(1,128)} %copy.44), calls=%async_computation | async-start | bytes 16384 | tf_op jit(solution)/shard_map/all_to_all | solution.py:67
  43.0 0.8 gather_fusion.1
  43.8 6.3 %scatter_fusion.3 = bf16[8,16,1920]{2,1,0:T(8,128)(2,1)S(1)} fusion(bf16[8,16,1920]{2,1,0:T(8,128)(2,1)S(1)} %broadcast_in_dim.12, s32[64]{0:T(128)S(1)} %fusion.25, bf16[64,1920]{1,0:T(8,128)(2,1)S(1)} %gather_fusion.1), kind=kCustom, calls=%fused_computation.6 | custom fusion | bytes 737792 | tf_op jit(solution)/shard_map/scatter | solution.py:56
  50.1 0.9 copy.51
  50.9 6.0 %all-to-all-start.3 = ((bf16[8,16,1920]{2,0,1:T(8,128)(2,1)}), bf16[8,16,1920]{2,0,1:T(8,128)(2,1)S(1)}, u32[]{:S(2)}, u32[]{:S(2)}) async-start(bf16[8,16,1920]{2,0,1:T(8,128)(2,1)} %copy.51), calls=%async_computation.3 | async-start | bytes 983040 | tf_op jit(solution)/shard_map/all_to_all | solution.py:64
  57.4 13.3 %all-to-all-done.3 = bf16[8,16,1920]{2,0,1:T(8,128)(2,1)S(1)} async-done(((bf16[8,16,1920]{2,0,1:T(8,128)(2,1)}), bf16[8,16,1920]{2,0,1:T(8,128)(2,1)S(1)}, u32[]{:S(2)}, u32[]{:S(2)}) %all-to-all-start.3) | async-done | bytes 491552 | tf_op jit(solution)/shard_map/all_to_all | solution.py:64
  70.8 4.0 %multiply_convert_fusion = bf16[8,16,1920]{2,1,0:T(8,128)(2,1)S(1)} fusion(f32[8,16,1920]{2,1,0:T(8,128)S(1)} %copy_convert_fusion, f32[8,16]{1,0:T(8,128)S(1)} %get-tuple-element.6, f32[8,16]{1,0:T(8,128)S(1)} %get-tuple-element.7, f32[8,16]{1,0:T(8,128)S(1)} %get-tuple-element.8, f32[8,16]{1,0:T(8,128)S(1)} %get-tuple-element.9, ...), kind=kLoop, calls=%fused_computation.7 | loop fusion | flops 7618560 | bytes 1479168 | tf_op jit(solution)/shard_map/convert_element_type | solution.py:69
  74.8 0.9 fusion.11
  75.8 20.8 %all-reduce.4.cloned.1.call-done = f32[16,1920]{1,0:T(8,128)} async-done(((f32[16,1920]{1,0:T(8,128)}), f32[16,1920]{1,0:T(8,128)}) %all-reduce.4.cloned.1.call-update) | async-done | bytes 122896 | tf_op jit(solution)/shard_map/psum | solution.py:79
  96.6 1.0 slice.83
  97.6 0.9 pad_maximum_fusion
  98.6 7.8 %copy.53 = f32[16,1920,2]{2,1,0:T(8,128)} copy(f32[16,1920,2]{1,0,2:T(8,128)S(1)} %pad_maximum_fusion) | data formatting | bytes 491520 | tf_op jit(solution)/shard_map/stack | solution.py:30
  106.3 118.6 %gather_fusion.2 = f32[8192,2]{1,0:T(8,128)} fusion(f32[16,1920,2]{2,1,0:T(8,128)} %copy.53, s32[8192]{0:T(1024)S(1)} %bitcast.70), kind=kCustom, calls=%fused_computation.2 | custom fusion | bytes 196608 | tf_op jit(solution)/shard_map/jit(take_along_axis)/gather | solution.py:31
  225.0 2.8 %copy.54 = f32[16,512,2]{1,0,2:T(8,128)S(1)} copy(f32[16,512,2]{2,1,0:T(8,128)} %bitcast.74) | data formatting | bytes 131072 | tf_op jit(solution)/shard_map/jit(take_along_axis)/gather | solution.py:31
  227.9 0.6 broadcast_multiply_fusion
  (33 shorter events, 1.0 us)
Async XLA Ops:
  6.5 36.4 %copy-start = (bf16[16,1920]{1,0:T(8,128)(2,1)S(1)}, bf16[16,1920]{1,0:T(8,128)(2,1)}, u32[]{:S(2)}) copy-start(bf16[16,1920]{1,0:T(8,128)(2,1)} %param.7) | copy-start | bytes 184324
  12.9 13.8 %all-to-all-start.1 = ((bf16[8,16,1]{0,2,1:T(2,128)(2,1)}), bf16[8,16,1]{0,2,1:T(2,128)(2,1)S(1)}, u32[]{:S(2)}, u32[]{:S(2)}) async-start(bf16[8,16,1]{0,2,1:T(2,128)(2,1)} %copy.47), calls=%async_computation.1 | async-start | bytes 16384 | tf_op jit(solution)/shard_map/all_to_all | solution.py:65
  26.7 11.6 %all-to-all-start.2 = ((s32[8,16,1]{0,2,1:T(1,128)}), s32[8,16,1]{0,2,1:T(1,128)S(1)}, u32[]{:S(2)}, u32[]{:S(2)}) async-start(s32[8,16,1]{0,2,1:T(1,128)} %copy.49), calls=%async_computation.2 | async-start | bytes 16384 | tf_op jit(solution)/shard_map/all_to_all | solution.py:66
  38.4 12.6 %all-to-all-start = ((s32[8,16,1]{0,2,1:T(1,128)}), s32[8,16,1]{0,2,1:T(1,128)S(1)}, u32[]{:S(2)}, u32[]{:S(2)}) async-start(s32[8,16,1]{0,2,1:T(1,128)} %copy.44), calls=%async_computation | async-start | bytes 16384 | tf_op jit(solution)/shard_map/all_to_all | solution.py:67
  43.0 14.0 %copy-start.1 = (f32[1,16,512]{2,1,0:T(8,128)S(1)}, f32[1,16,512]{2,1,0:T(8,128)}, u32[]{:S(2)}) copy-start(f32[1,16,512]{2,1,0:T(8,128)} %param.12) | copy-start | bytes 98308
  50.9 19.8 %all-to-all-start.3 = ((bf16[8,16,1920]{2,0,1:T(8,128)(2,1)}), bf16[8,16,1920]{2,0,1:T(8,128)(2,1)S(1)}, u32[]{:S(2)}, u32[]{:S(2)}) async-start(bf16[8,16,1920]{2,0,1:T(8,128)(2,1)} %copy.51), calls=%async_computation.3 | async-start | bytes 983040 | tf_op jit(solution)/shard_map/all_to_all | solution.py:64
  56.9 39.7 %all-reduce.4.cloned.1.call-start = ((), (), s32[]{:S(2)}) async-start(), calls=%async_computation.4 | async-start | bytes 245760 | tf_op jit(solution)/shard_map/psum | solution.py:79
  225.0 2.9 %copy-start.2 = (f32[1,16,512]{2,1,0:T(8,128)S(1)}, f32[1,16,512]{2,1,0:T(8,128)}, u32[]{:S(2)}) copy-start(f32[1,16,512]{2,1,0:T(8,128)} %param.13) | copy-start | bytes 98308
Sparse Core Ops, SparseCore 0:
  75.9 20.6 all-reduce.3
where the time goes:
time: 236 us; the launch traced here: 235 us
  local copies, waits for them, and re-layouts  155 us (66%)
  waiting for transfers between devices  36.4 us (15%)
  starting transfers between devices  23.2 us (10%)
  between operations  13.6 us (6%)
  other arithmetic  6.02 us (3%)
    gather x2, local copies, waits for them, and re-layouts, interpolate(): picked = jnp.take_along_axis(paired, lower_index[:, :, None], axis=1)  121 us
    psum x1, waiting for transfers between devices, per_device(): summed_stack = lax.psum(stack, 'table')  20.8 us
    all_to_all x1, waiting for transfers between devices, per_device(): lax.all_to_all(raw_slots, 'image', split_axis=1, concat_axis=1, tiled=True)  13.3 us
    another operation x2, local copies, waits for them, and re-layouts, interpolate(): paired = jnp.stack([stack_tile, shifted], axis=-1)  7.79 us
    all_to_all x1, starting transfers between devices, per_device(): lax.all_to_all(gain_slots, 'image', split_axis=1, concat_axis=1, tiled=True)  7.39 us
    scatter x2, local copies, waits for them, and re-layouts, per_device(): raw_slots = jnp.zeros((capacity, tiles, samples), jnp.bfloat16).at[slot_i...  7.14 us
    scatter x2, local copies, waits for them, and re-layouts, per_device(): jnp.zeros((capacity, tiles), jnp.int32).at[slot_index, destination]  6.91 us
    all_to_all x1, starting transfers between devices, per_device(): lax.all_to_all(raw_slots, 'image', split_axis=1, concat_axis=1, tiled=True)  6.01 us
  transfers between devices with their start and end apart: 5, of which 4 were waited for; matrix products, arithmetic and copies ran while one was open for 8% of the time, Pallas kernels for 0%

commit v1 on v0

--- a/solution.py
+++ b/solution.py
@@ -76,7 +76,8 @@
         node_member, flat_values, (((0,), (0,)), ((), ())), preferred_element_type=jnp.float32
     )
     scale = 1.0 / math.sqrt(trace_count * groups * aper_count)
-    summed_stack = lax.psum(stack, "table")
+    blocks = lax.all_gather(stack, "table")
+    summed_stack = jnp.sum(blocks, axis=0)
     return (interpolate(summed_stack, travel[0], spread[0]) * scale)[None, :]
 
 

time: 236 us -> 206 us (0.87)
  waiting for transfers between devices: 36.4 us -> 15.6 us
  between operations: 13.6 us -> 0.24 us
  blocking collectives: 0 us -> 6.02 us
    psum x1 -> x0, waiting for transfers between devices: 20.8 us -> none  [per_device(): summed_stack = lax.psum(stack, 'table')]
    all_gather x0 -> x1, blocking collectives: none -> 6.02 us  [per_device(): blocks = lax.all_gather(stack, 'table')]
  transfers between devices with their start and end apart: 5 -> 4, of which waited for: 4 -> 3; matrix products, arithmetic and copies ran while one was open for 8% -> 9% of each run, Pallas kernels for 0% -> 0%
where the time goes in v1:
time: 206 us; the launch traced here: 205 us
  local copies, waits for them, and re-layouts  154 us (75%)
  starting transfers between devices  23.2 us (11%)
  waiting for transfers between devices  15.6 us (8%)
  blocking collectives  6.02 us (3%)
  other arithmetic  5.14 us (2%)
    gather x2, local copies, waits for them, and re-layouts, interpolate(): picked = jnp.take_along_axis(paired, lower_index[:, :, None], axis=1)  121 us
    all_to_all x1, waiting for transfers between devices, per_device(): lax.all_to_all(raw_slots, 'image', split_axis=1, concat_axis=1, tiled=True)  13.4 us
    another operation x2, local copies, waits for them, and re-layouts, interpolate(): paired = jnp.stack([stack_tile, shifted], axis=-1)  7.79 us
    all_to_all x1, starting transfers between devices, per_device(): lax.all_to_all(gain_slots, 'image', split_axis=1, concat_axis=1, tiled=True)  7.39 us
    scatter x2, local copies, waits for them, and re-layouts, per_device(): raw_slots = jnp.zeros((capacity, tiles, samples), jnp.bfloat16).at[slot_i...  7.14 us
    scatter x2, local copies, waits for them, and re-layouts, per_device(): jnp.zeros((capacity, tiles), jnp.int32).at[slot_index, destination]  6.91 us
    all_gather x1, blocking collectives, per_device(): blocks = lax.all_gather(stack, 'table')  6.02 us
    all_to_all x1, starting transfers between devices, per_device(): lax.all_to_all(raw_slots, 'image', split_axis=1, concat_axis=1, tiled=True)  6.01 us
  transfers between devices with their start and end apart: 4, of which 3 were waited for; matrix products, arithmetic and copies ran while one was open for 9% of the time, Pallas kernels for 0%

profile of v1, /device:TPU:0, one launch (start us, length us, event | category | flops | bytes accessed | tf_op | source)
XLA Modules:
  0.0 204.6 jit_solution(5882503533904131724)
XLA Ops:
  0.0 0.8 copy.48
  0.9 0.1 reshape.171
  1.0 0.1 reduce_window_sum.11
  1.1 0.2 select_reduce_fusion
  1.3 0.8 copy.53
  2.1 0.1 reshape.206
  2.2 3.5 %scatter_fusion.1 = bf16[8,16]{1,0:T(8,128)(2,1)S(1)} fusion(bf16[8,16]{1,0:T(8,128)(2,1)S(1)} %broadcast_in_dim.11, s32[64]{0:T(128)S(1)} %fusion.25, bf16[64]{0:T(256)(128)(2,1)S(1)} %reshape.206), kind=kCustom, calls=%fused_computation.4 | custom fusion | bytes 896 | tf_op jit(solution)/shard_map/scatter | solution.py:59
  5.7 0.7 copy.54
  6.4 7.4 %all-to-all-start.1 = ((bf16[8,16,1]{0,2,1:T(2,128)(2,1)}), bf16[8,16,1]{0,2,1:T(2,128)(2,1)S(1)}, u32[]{:S(2)}, u32[]{:S(2)}) async-start(bf16[8,16,1]{0,2,1:T(2,128)(2,1)} %copy.54), calls=%async_computation.1 | async-start | bytes 16384 | tf_op jit(solution)/shard_map/all_to_all | solution.py:65
  13.8 1.4 gather_fusion
  15.3 3.5 %scatter_fusion.2 = s32[8,16]{1,0:T(8,128)S(1)} fusion(s32[8,16]{1,0:T(8,128)S(1)} %broadcast.222.clone, s32[64]{0:T(128)S(1)} %fusion.25, s32[64]{0:T(128)S(1)} %gather_fusion), kind=kCustom, calls=%fused_computation.5 | custom fusion | bytes 1280 | tf_op jit(solution)/shard_map/scatter | solution.py:62
  18.7 0.7 copy.56
  19.4 0.8 all-to-all-done.1
  20.2 5.2 %all-to-all-start.2 = ((s32[8,16,1]{0,2,1:T(1,128)}), s32[8,16,1]{0,2,1:T(1,128)S(1)}, u32[]{:S(2)}, u32[]{:S(2)}) async-start(s32[8,16,1]{0,2,1:T(1,128)} %copy.56), calls=%async_computation.2 | async-start | bytes 16384 | tf_op jit(solution)/shard_map/all_to_all | solution.py:66
  25.4 0.8 copy.50
  26.3 3.5 %scatter_fusion = s32[8,16]{1,0:T(8,128)S(1)} fusion(s32[8,16]{1,0:T(8,128)S(1)} %broadcast.222.clone.1, s32[64]{0:T(128)S(1)} %fusion.25, s32[64]{0:T(128)S(1)} %reshape.200), kind=kCustom, calls=%fused_computation.3 | custom fusion | bytes 1280 | tf_op jit(solution)/shard_map/scatter | solution.py:52
  29.7 0.7 copy.51
  30.4 1.4 all-to-all-done.2
  31.8 4.6 %all-to-all-start = ((s32[8,16,1]{0,2,1:T(1,128)}), s32[8,16,1]{0,2,1:T(1,128)S(1)}, u32[]{:S(2)}, u32[]{:S(2)}) async-start(s32[8,16,1]{0,2,1:T(1,128)} %copy.51), calls=%async_computation | async-start | bytes 16384 | tf_op jit(solution)/shard_map/all_to_all | solution.py:67
  36.4 0.8 gather_fusion.1
  37.2 6.3 %scatter_fusion.3 = bf16[8,16,1920]{2,1,0:T(8,128)(2,1)S(1)} fusion(bf16[8,16,1920]{2,1,0:T(8,128)(2,1)S(1)} %broadcast_in_dim.12, s32[64]{0:T(128)S(1)} %fusion.25, bf16[64,1920]{1,0:T(8,128)(2,1)S(1)} %gather_fusion.1), kind=kCustom, calls=%fused_computation.6 | custom fusion | bytes 737792 | tf_op jit(solution)/shard_map/scatter | solution.py:56
  43.5 0.9 copy.58
  44.4 6.0 %all-to-all-start.3 = ((bf16[8,16,1920]{2,0,1:T(8,128)(2,1)}), bf16[8,16,1920]{2,0,1:T(8,128)(2,1)S(1)}, u32[]{:S(2)}, u32[]{:S(2)}) async-start(bf16[8,16,1920]{2,0,1:T(8,128)(2,1)} %copy.58), calls=%async_computation.3 | async-start | bytes 983040 | tf_op jit(solution)/shard_map/all_to_all | solution.py:64
  50.8 13.4 %all-to-all-done.3 = bf16[8,16,1920]{2,0,1:T(8,128)(2,1)S(1)} async-done(((bf16[8,16,1920]{2,0,1:T(8,128)(2,1)}), bf16[8,16,1920]{2,0,1:T(8,128)(2,1)S(1)}, u32[]{:S(2)}, u32[]{:S(2)}) %all-to-all-start.3) | async-done | bytes 491552 | tf_op jit(solution)/shard_map/all_to_all | solution.py:64
  64.3 4.0 %multiply_convert_fusion = bf16[8,16,1920]{2,1,0:T(8,128)(2,1)S(1)} fusion(f32[8,16,1920]{2,1,0:T(8,128)S(1)} %copy_convert_fusion, f32[8,16]{1,0:T(8,128)S(1)} %get-tuple-element.6, f32[8,16]{1,0:T(8,128)S(1)} %get-tuple-element.7, f32[8,16]{1,0:T(8,128)S(1)} %get-tuple-element.8, f32[8,16]{1,0:T(8,128)S(1)} %get-tuple-element.9, ...), kind=kLoop, calls=%fused_computation.7 | loop fusion | flops 7618560 | bytes 1479168 | tf_op jit(solution)/shard_map/convert_element_type | solution.py:69
  68.2 0.3 fusion.11
  68.5 6.0 %all-gather = f32[32,1920]{1,0:T(8,128)S(1)} all-gather(f32[16,1920]{1,0:T(8,128)S(1)} %fusion.11), channel_id=2, replica_groups=mesh['table'=2,'image'=16] {'table'}, dimensions={0}, use_global_device_ids=true | all-gather | bytes 368640 | tf_op jit(solution)/shard_map/all_gather | solution.py:79
  74.6 0.1 slice.83
  74.7 7.8 %copy.60 = f32[16,1920,2]{2,1,0:T(8,128)} copy(f32[16,1920,2]{1,0,2:T(8,128)S(1)} %pad_maximum_fusion) | data formatting | bytes 491520 | tf_op jit(solution)/shard_map/stack | solution.py:30
  82.5 118.6 %gather_fusion.2 = f32[8192,2]{1,0:T(8,128)} fusion(f32[16,1920,2]{2,1,0:T(8,128)} %copy.60, s32[8192]{0:T(1024)S(1)} %bitcast.71), kind=kCustom, calls=%fused_computation.2 | custom fusion | bytes 196608 | tf_op jit(solution)/shard_map/jit(take_along_axis)/gather | solution.py:31
  201.1 2.8 %copy.61 = f32[16,512,2]{1,0,2:T(8,128)S(1)} copy(f32[16,512,2]{2,1,0:T(8,128)} %bitcast.75) | data formatting | bytes 131072 | tf_op jit(solution)/shard_map/jit(take_along_axis)/gather | solution.py:31
  204.0 0.6 broadcast_multiply_fusion
  (32 shorter events, 0.9 us)
Async XLA Ops:
  0.0 36.4 %copy-start = (bf16[16,1920]{1,0:T(8,128)(2,1)S(1)}, bf16[16,1920]{1,0:T(8,128)(2,1)}, u32[]{:S(2)}) copy-start(bf16[16,1920]{1,0:T(8,128)(2,1)} %param.7) | copy-start | bytes 184324
  6.4 13.8 %all-to-all-start.1 = ((bf16[8,16,1]{0,2,1:T(2,128)(2,1)}), bf16[8,16,1]{0,2,1:T(2,128)(2,1)S(1)}, u32[]{:S(2)}, u32[]{:S(2)}) async-start(bf16[8,16,1]{0,2,1:T(2,128)(2,1)} %copy.54), calls=%async_computation.1 | async-start | bytes 16384 | tf_op jit(solution)/shard_map/all_to_all | solution.py:65
  20.2 11.6 %all-to-all-start.2 = ((s32[8,16,1]{0,2,1:T(1,128)}), s32[8,16,1]{0,2,1:T(1,128)S(1)}, u32[]{:S(2)}, u32[]{:S(2)}) async-start(s32[8,16,1]{0,2,1:T(1,128)} %copy.56), calls=%async_computation.2 | async-start | bytes 16384 | tf_op jit(solution)/shard_map/all_to_all | solution.py:66
  31.8 12.6 %all-to-all-start = ((s32[8,16,1]{0,2,1:T(1,128)}), s32[8,16,1]{0,2,1:T(1,128)S(1)}, u32[]{:S(2)}, u32[]{:S(2)}) async-start(s32[8,16,1]{0,2,1:T(1,128)} %copy.51), calls=%async_computation | async-start | bytes 16384 | tf_op jit(solution)/shard_map/all_to_all | solution.py:67
  36.4 14.0 %copy-start.1 = (f32[1,16,512]{2,1,0:T(8,128)S(1)}, f32[1,16,512]{2,1,0:T(8,128)}, u32[]{:S(2)}) copy-start(f32[1,16,512]{2,1,0:T(8,128)} %param.12) | copy-start | bytes 98308
  44.4 19.8 %all-to-all-start.3 = ((bf16[8,16,1920]{2,0,1:T(8,128)(2,1)}), bf16[8,16,1920]{2,0,1:T(8,128)(2,1)S(1)}, u32[]{:S(2)}, u32[]{:S(2)}) async-start(bf16[8,16,1920]{2,0,1:T(8,128)(2,1)} %copy.58), calls=%async_computation.3 | async-start | bytes 983040 | tf_op jit(solution)/shard_map/all_to_all | solution.py:64
  201.1 2.9 %copy-start.2 = (f32[1,16,512]{2,1,0:T(8,128)S(1)}, f32[1,16,512]{2,1,0:T(8,128)}, u32[]{:S(2)}) copy-start(f32[1,16,512]{2,1,0:T(8,128)} %param.13) | copy-start | bytes 98308
